TPU v7x, 256 devices: a whole 4x4x8 slice. The times are simulated.
256 devices in a mesh: gx: 8 (over z), gy: 32 (over x, y, core).
Axes of the slice: x: 4, y: 4, z: 8, core: 2. Of those that a mesh axis runs over, the one named last changes fastest.
Arguments:
- data: bfloat16 [128, 1024, 4096], P(None, 'gx', 'gy')
- inv_scale: float32 [128], replicated, may hold values from 0.1 to 1
- start: float32 [128, 32], replicated, may hold values from -6 to 6
- rank: int32 [1], replicated, may hold values from 24 to 32
Outputs:
- core: bfloat16 [32, 1024, 4096], P(None, 'gx', 'gy')
- factor: float32 [128, 32], replicated
Inputs may be any that keep to these rules, and one draw needn't show every extreme that they name: rank[0] is the number of leading columns of the factor that are kept.
All inputs are finite; a program needn't handle non-finite values.
Results may differ from a plain program's by a relative error of at most 0.0044.
Values sent between devices are 32-bit elements; how exact they have to be, the bound alone decides.
No kernel may reach another device: no remote copies, remote signals or barrier semaphores. Data moves between devices by JAX's collectives and lax.ppermute only.
A program may use at most 64 MiB of HBM per device.

v0:
```python
import jax
import jax.numpy as jnp
from jax import lax
from jax.sharding import PartitionSpec as P

ITERS = 4


def body(data, inv_scale, start, rank):
    variables = data.shape[0]
    columns = start.shape[1]
    flat = data.reshape(variables, -1)
    local_gram = lax.dot_general(
        flat, flat, (((1,), (1,)), ((), ())), preferred_element_type=jnp.float32
    )
    gram = lax.psum(local_gram, ("gx", "gy"))
    weighted = inv_scale[:, None] * gram * inv_scale[None, :]
    basis = start
    for turn in range(ITERS):
        image = jnp.dot(weighted, basis, precision=lax.Precision.HIGHEST)
        inner = jnp.dot(image.T, image, precision=lax.Precision.HIGHEST)
        lower = jnp.linalg.cholesky(inner)
        basis = lax.linalg.triangular_solve(
            lower, image, left_side=False, lower=True, transpose_a=True
        )
    keep = (jnp.arange(columns, dtype=jnp.int32) < rank[0]).astype(jnp.float32)
    factor = basis * keep[None, :]
    scaled_factor = (inv_scale[:, None] * factor).astype(jnp.bfloat16)
    product = lax.dot_general(
        scaled_factor, flat, (((0,), (0,)), ((), ())), preferred_element_type=jnp.float32
    )
    core = product.astype(jnp.bfloat16).reshape(columns, data.shape[1], data.shape[2])
    return (core, factor)


def solution(mesh):
    in_specs = (P(None, "gx", "gy"), P(), P(), P())
    out_specs = (P(None, "gx", "gy"), P())
    return jax.shard_map(body, mesh=mesh, in_specs=in_specs, out_specs=out_specs, check_vma=False)
```

profile of v0, /device:TPU:1, one launch (start us, length us, event | category | flops | bytes accessed | tf_op | source)
XLA Modules:
  0.0 304.1 jit_solution(8816797519067083636)
XLA Ops:
  7.2 0.0 copy-start
  7.2 0.0 copy-start.1
  7.2 0.0 all-reduce.2.cloned.1.call-start
  7.2 8.8 %fusion.7 = f32[128,128]{1,0:T(8,128)} fusion(bf16[128,128,128]{2,1,0:T(8,128)(2,1)} %param.7), kind=kOutput, calls=%fused_computation.6 | convolution fusion | flops 536870912 | bytes 4259840 | tf_op jit(solution)/shard_map/dot_general | solution.py:13
  16.0 0.0 all-reduce.2.cloned.1.call-update
  16.7 241.3 %all-reduce.2.cloned.1.call-done = f32[128,128]{1,0:T(8,128)} async-done(((f32[128,128]{1,0:T(8,128)}), f32[128,128]{1,0:T(8,128)}) %all-reduce.2.cloned.1.call-update) | async-done | bytes 65552 | tf_op jit(solution)/shard_map/psum | solution.py:16
  258.0 0.0 copy-done
  258.0 0.0 copy-done.1
  258.0 1.1 fusion.14
  259.1 0.2 fusion.42
  259.3 0.1 copy.8
  259.4 2.9 cholesky.74
  262.3 0.6 compare_reduce_fusion.3
  263.0 0.7 fusion.23
  263.6 2.4 custom-call.8
  266.1 0.2 convolution_bitcast_fusion.3
  266.3 1.1 fusion.13
  267.4 0.2 fusion.43
  267.6 0.1 copy.9
  267.7 2.9 cholesky.85
  270.6 0.6 compare_reduce_fusion.2
  271.3 0.7 fusion.24
  271.9 2.4 custom-call.9
  274.4 0.2 convolution_bitcast_fusion.2
  274.6 1.1 fusion.12
  275.7 0.2 fusion.44
  275.9 0.1 copy.10
  276.0 2.9 cholesky.96
  279.0 0.6 compare_reduce_fusion.1
  279.6 0.7 fusion.25
  280.3 2.4 custom-call.10
  282.7 0.2 convolution_bitcast_fusion.1
  282.9 1.1 fusion.11
  284.0 0.2 fusion.45
  284.2 0.1 copy.11
  284.3 2.9 cholesky.107
  287.3 0.6 compare_reduce_fusion
  287.9 0.7 fusion.26
  288.6 2.4 custom-call.11
  291.0 0.2 fusion.10
  291.2 0.0 copy-start.2
  291.3 4.8 %fusion.4 = bf16[4,8,128,128]{3,1,2,0:T(8,128)(2,1)S(1)} fusion(bf16[16,8,128,128]{3,2,1,0:T(8,128)(2,1)} %bitcast.75, f32[128,32]{0,1:T(8,128)S(1)} %fusion.10, f32[128]{0:T(128)S(1)} %copy-done.1), kind=kOutput, calls=%fused_computation.5 | convolution fusion | flops 134750208 | bytes 5259776 | tf_op jit(solution)/shard_map/dot_general | solution.py:29
  296.1 1.2 copy.13
  297.3 0.0 copy-done.2
  (9 shorter events, 0.2 us)
Async XLA Ops:
  7.2 250.8 %copy-start = (f32[128,32]{0,1:T(8,128)S(1)}, f32[128,32]{0,1:T(8,128)}, u32[]{:S(2)}) copy-start(f32[128,32]{0,1:T(8,128)} %param.9) | copy-start | bytes 49156
  7.2 250.8 %copy-start.1 = (f32[128]{0:T(128)S(1)}, f32[128]{0:T(128)}, u32[]{:S(2)}) copy-start(f32[128]{0:T(128)} %param.8) | copy-start | bytes 1540
  7.2 250.8 %all-reduce.2.cloned.1.call-start = ((), (), s32[]{:S(2)}) async-start(), calls=%async_computation | async-start | bytes 131072 | tf_op jit(solution)/shard_map/psum | solution.py:16
  291.2 6.0 %copy-start.2 = (f32[128,32]{0,1:T(8,128)}, f32[128,32]{0,1:T(8,128)S(1)}, u32[]{:S(2)}) copy-start(f32[128,32]{0,1:T(8,128)S(1)} %fusion.10) | copy-start | bytes 49156
Sparse Core Ops, SparseCore 0:
  16.1 241.8 all-reduce.1
where the time goes:
time: 304 us
  waiting for transfers between devices  241 us (79%)
  other arithmetic  26.8 us (9%)
  matrix products  19.6 us (6%)
  between operations  14.9 us (5%)
    psum x1, waiting for transfers between devices, body(): gram = lax.psum(local_gram, ('gx', 'gy'))  241 us
    another operation x12, other arithmetic, body(): lower = jnp.linalg.cholesky(inner)  14.4 us
    another operation x8, other arithmetic, body(): lax.linalg.triangular_solve(lower, image, left_side=False, lower=True, tr...  12.3 us
    dot_general x1, matrix products, body(): lax.dot_general(flat, flat, (((1,), (1,)), ((), ())), preferred_element_t...  8.76 us
  transfers between devices with their start and end apart: 1, of which 1 were waited for; matrix products, arithmetic and copies ran while one was open for 0% of the time, Pallas kernels for 0%

commit v1 on v0

v1 whole, which is shorter than its diff:
```python
import functools

import jax
import jax.numpy as jnp
from jax import lax
from jax.experimental import pallas as pl
from jax.experimental.pallas import tpu as pltpu
from jax.sharding import PartitionSpec as P

ITERS = 4
VMEM = pl.BlockSpec(memory_space=pltpu.VMEM)
SMEM = pl.BlockSpec(memory_space=pltpu.SMEM)
SMALL = pltpu.CompilerParams(vmem_limit_bytes=4 * 2**20)


def split3(x):
    a = x.astype(jnp.bfloat16)
    rest = x - a.astype(jnp.float32)
    b = rest.astype(jnp.bfloat16)
    c = (rest - b.astype(jnp.float32)).astype(jnp.bfloat16)
    return a, b, c


def iota(shape, dim):
    return lax.broadcasted_iota(jnp.int32, shape, dim)


def pack_kernel(gram_ref, out_ref):
    v = gram_ref.shape[0]
    h = v // 2
    gram = gram_ref[...]
    lower_right = pltpu.roll(gram[h:], h, 1)
    row, col = iota((h, v), 0), iota((h, v), 1)
    out_ref[:h] = jnp.where((col >= h) | (row >= col), gram[:h], lower_right)
    diagonal = jnp.sum(jnp.where(iota((v, v), 0) == iota((v, v), 1), gram, 0.0), axis=0, keepdims=True)
    out_ref[h:] = jnp.broadcast_to(diagonal, (out_ref.shape[0] - h, v))


def unpack(packed, v):
    h = v // 2
    q = jnp.concatenate([packed[:h], packed[:h]], axis=0)
    qt = q.T
    row, col = iota((v, v), 0), iota((v, v), 1)
    top = jnp.where((col >= h) | (row >= col), q, qt)
    shifted = pltpu.roll(q, h, 1)
    shifted_t = jnp.concatenate([qt[h:], qt[:h]], axis=0)
    corner = jnp.where(row < col, shifted, shifted_t)
    corner = jnp.where(row == col, packed[h : h + 1], corner)
    bottom = jnp.where(col < h, qt, corner)
    return jnp.where(row < h, top, bottom)


def pair_kernel(a_ref, b_ref, out_ref):
    total = a_ref[...] + b_ref[...]
    for n in range(out_ref.shape[0]):
        out_ref[n] = total


def many_kernel(in_ref, out_ref):
    total = in_ref[0]
    for n in range(1, in_ref.shape[0]):
        total = total + in_ref[n]
    for n in range(out_ref.shape[0]):
        out_ref[n] = total


def eliminate(inner, image, out_ref):
    k_max = inner.shape[0]
    blocks = k_max // 8
    a = [inner[8 * n : 8 * n + 8] for n in range(blocks)]
    y = [image[8 * n : 8 * n + 8] for n in range(blocks)]
    below = iota((8, 1), 0)
    for k in range(k_max):
        b, s = divmod(k, 8)
        row = a[b][s : s + 1]
        r = lax.rsqrt(row[:, k : k + 1])
        ua = row * r
        uy = y[b][s : s + 1] * r
        out_ref[k : k + 1, :] = uy
        for c in range(b, blocks):
            m = a[c][:, k : k + 1] * r
            if c == b:
                m = jnp.where(below > s, m, 0.0)
            a[c] = a[c] - m * ua
            y[c] = y[c] - m * uy


def iterate_kernel(rank_ref, parts_ref, scale_ref, start_ref, factor_ref, scaled_ref, g_ref, basis_ref):
    v = scale_ref.shape[1]
    packed = parts_ref[0]
    for n in range(1, parts_ref.shape[0]):
        packed = packed + parts_ref[n]
    g1, g2, g3 = split3(unpack(packed, v))
    for n, piece in enumerate((g1, g2, g1, g3, g2, g1)):
        g_ref[n * v : (n + 1) * v] = piece
    scale = scale_ref[...]
    basis = start_ref[...]
    for turn in range(ITERS):
        x1, x2, x3 = split3(basis * scale)
        x = jnp.concatenate([x1, x1, x2, x1, x2, x3], axis=1)
        image = jnp.dot(x, g_ref[...], preferred_element_type=jnp.float32) * scale
        y1, y2, y3 = split3(image)
        left = jnp.concatenate([y1, y1, y2, y1, y2, y3], axis=1)
        right = jnp.concatenate([y1, y2, y1, y3, y2, y1], axis=1)
        inner = lax.dot_general(left, right, (((1,), (1,)), ((), ())), preferred_element_type=jnp.float32)
        eliminate(inner, image, basis_ref)
        basis = basis_ref[...]
    factor = jnp.where(iota(basis.shape, 0) < rank_ref[0], basis, 0.0)
    factor_ref[...] = factor
    scaled_ref[...] = (factor * scale).astype(jnp.bfloat16)


def f32(*shape):
    return jax.ShapeDtypeStruct(shape, jnp.float32)


def body(data, inv_scale, start, rank):
    variables, columns = start.shape
    flat = data.reshape(variables, -1)
    gram = lax.dot_general(
        flat, flat, (((1,), (1,)), ((), ())), preferred_element_type=jnp.float32
    )
    rows = variables // 2 + 8
    nx, ny = lax.axis_size("gx"), lax.axis_size("gy")
    packed = pl.pallas_call(
        pack_kernel, out_shape=f32(rows, variables), in_specs=[VMEM], out_specs=VMEM, compiler_params=SMALL
    )(gram)
    other = lax.ppermute(packed, "gy", [(i, i ^ 1) for i in range(ny)])
    cores = [[2 * i + c for i in range(ny // 2)] for c in range(2)]
    sent = pl.pallas_call(
        pair_kernel, out_shape=f32(ny // 2, rows, variables), in_specs=[VMEM] * 2, out_specs=VMEM, compiler_params=SMALL
    )(packed, other)
    got = lax.all_to_all(sent, "gy", 0, 0, axis_index_groups=cores)
    sent = pl.pallas_call(
        many_kernel, out_shape=f32(nx, rows, variables), in_specs=[VMEM], out_specs=VMEM, compiler_params=SMALL
    )(got)
    got = lax.all_to_all(sent, "gx", 0, 0)
    factor_t, scaled_t = pl.pallas_call(
        iterate_kernel,
        out_shape=(f32(columns, variables), jax.ShapeDtypeStruct((columns, variables), jnp.bfloat16)),
        in_specs=[SMEM, VMEM, VMEM, VMEM],
        out_specs=(VMEM, VMEM),
        compiler_params=SMALL,
        scratch_shapes=[
            pltpu.VMEM((6 * variables, variables), jnp.bfloat16),
            pltpu.VMEM((columns, variables), jnp.float32),
        ],
    )(rank, got, inv_scale[None, :], start.T)
    product = lax.dot_general(
        scaled_t, flat, (((1,), (0,)), ((), ())), preferred_element_type=jnp.float32
    )
    core = product.astype(jnp.bfloat16).reshape(columns, data.shape[1], data.shape[2])
    return (core, factor_t.T)


def solution(mesh):
    in_specs = (P(None, "gx", "gy"), P(), P(), P())
    out_specs = (P(None, "gx", "gy"), P())
    return jax.shard_map(body, mesh=mesh, in_specs=in_specs, out_specs=out_specs, check_vma=False)
```

time: 304 us -> 68 us (0.22)
  waiting for transfers between devices: 241 us -> 10.2 us
  other arithmetic: 26.8 us -> 0 us
  blocking collectives: 0 us -> 16.3 us
  between operations: 14.9 us -> 1.32 us
  Pallas kernels: 0 us -> 13.2 us
  starting transfers between devices: 0.04 us -> 11.5 us
  matrix products: 19.6 us -> 12.9 us
    psum x1 -> x0, waiting for transfers between devices: 241 us -> none  [body(): gram = lax.psum(local_gram, ('gx', 'gy'))]
    another operation x20 -> x0, other arithmetic: 26.7 us -> none  [the longest x12 14.4 us: body(): lower = jnp.linalg.cholesky(inner)]
    all_to_all x0 -> x1, blocking collectives: none -> 16.3 us  [body(): got = lax.all_to_all(sent, 'gy', 0, 0, axis_index_groups=cores)]
    pallas_call x0 -> x4, Pallas kernels: none -> 13.2 us  [the longest x1 12.3 us: body(): pl.pallas_call(iterate_kernel, out_shape=(f32(columns, variables), jax.Sh...]
    all_to_all x0 -> x1, waiting for transfers between devices: none -> 9.34 us  [body(): got = lax.all_to_all(sent, 'gx', 0, 0)]
    all_to_all x0 -> x1, starting transfers between devices: none -> 8.19 us  [body(): got = lax.all_to_all(sent, 'gx', 0, 0)]
    dot_general x9 -> x1, matrix products: 9.89 us -> 4.82 us  [body(): lax.dot_general(scaled_t, flat, (((1,), (0,)), ((), ())), preferred_eleme...]
    ppermute x0 -> x1, starting transfers between devices: none -> 3.29 us  [body(): other = lax.ppermute(packed, 'gy', [(i, i ^ 1) for i in range(ny)])]
  transfers between devices with their start and end apart: 1 -> 2, of which waited for: 1 -> 2; matrix products, arithmetic and copies ran while one was open for 0% -> 0% of each run, Pallas kernels for 0% -> 0%
where the time goes in v1:
time: 68 us; the launch traced here: 66.7 us
  blocking collectives  16.3 us (24%)
  Pallas kernels  13.2 us (19%)
  matrix products  12.9 us (19%)
  starting transfers between devices  11.5 us (17%)
  waiting for transfers between devices  10.2 us (15%)
  between operations  1.32 us (2%)
  local copies, waits for them, and re-layouts  1.21 us (2%)
    all_to_all x1, blocking collectives, body(): got = lax.all_to_all(sent, 'gy', 0, 0, axis_index_groups=cores)  16.3 us
    pallas_call x1, Pallas kernels, body(): pl.pallas_call(iterate_kernel, out_shape=(f32(columns, variables), jax.Sh...  12.3 us
    all_to_all x1, waiting for transfers between devices, body(): got = lax.all_to_all(sent, 'gx', 0, 0)  9.34 us
    all_to_all x1, starting transfers between devices, body(): got = lax.all_to_all(sent, 'gx', 0, 0)  8.19 us
    dot_general x1, matrix products, body(): lax.dot_general(flat, flat, (((1,), (1,)), ((), ())), preferred_element_t...  8.12 us
    dot_general x1, matrix products, body(): lax.dot_general(scaled_t, flat, (((1,), (0,)), ((), ())), preferred_eleme...  4.82 us
    ppermute x1, starting transfers between devices, body(): other = lax.ppermute(packed, 'gy', [(i, i ^ 1) for i in range(ny)])  3.29 us
  transfers between devices with their start and end apart: 2, of which 2 were waited for; matrix products, arithmetic and copies ran while one was open for 0% of the time, Pallas kernels for 0%

profile of v1, /device:TPU:1, one launch (start us, length us, event | category | flops | bytes accessed | tf_op | source)
XLA Modules:
  0.0 66.7 jit_solution(2694978541148138433)
XLA Ops:
  0.6 0.0 copy-start
  0.6 0.0 copy-start.1
  0.6 8.1 %fusion.7.gram_ref = f32[128,128]{1,0:T(8,128)S(1)} fusion(bf16[128,128,128]{2,1,0:T(8,128)(2,1)} %param.4), kind=kOutput, calls=%fused_computation.6 | convolution fusion | flops 536870912 | bytes 4259840 | tf_op jit(solution)/shard_map/dot_general | solution.py:120
  8.8 0.1 shard_map.59.a_ref
  8.9 3.3 %collective-permute-start = (f32[72,128]{1,0:T(8,128)S(1)}, f32[72,128]{1,0:T(8,128)S(1)}, u32[]{:S(2)}, u32[]{:S(2)}) collective-permute-start(f32[72,128]{1,0:T(8,128)S(1)} %shard_map.59.a_ref), channel_id=1, source_target_pairs={{0,1},{1,0},{2,3},{3,2},{4,5},{5,4},{6,7},{7,6},{8,9},{9,8},{10,11... | collective-permute-start | bytes 110600 | tf_op jit(solution)/shard_map/ppermute | solution.py:128
  12.2 0.9 %collective-permute-done.b_ref = f32[72,128]{1,0:T(8,128)S(1)} collective-permute-done((f32[72,128]{1,0:T(8,128)S(1)}, f32[72,128]{1,0:T(8,128)S(1)}, u32[]{:S(2)}, u32[]{:S(2)}) %collective-permute-start) | collective-permute-done | bytes 36896 | tf_op jit(solution)/shard_map/ppermute | solution.py:128
  13.1 16.3 %all_to_all.10.in_ref = f32[16,72,128]{2,1,0:T(8,128)S(1)} all-to-all(f32[16,72,128]{2,1,0:T(8,128)S(1)} %shard_map.60), channel_id=1, replica_groups={{0,2,4,6,8,10,12,14,16,18,20,22,24,26,28,30},{1,3,5,7,9,11,13,15,17,19,..., dimensions={0} | all-to-all | bytes 1179648 | tf_op jit(solution)/shard_map/all_to_all | solution.py:133
  29.4 0.8 %shard_map.61 = f32[8,72,128]{2,1,0:T(8,128)} custom-call(f32[16,72,128]{2,1,0:T(8,128)S(1)} %all_to_all.10.in_ref), custom_call_target="tpu_custom_call" | custom-call | tf_op jit(solution)/shard_map/pallas_call | solution.py:134
  30.1 8.2 %all-to-all-start.1 = ((f32[8,72,128]{2,1,0:T(8,128)}), f32[8,72,128]{2,1,0:T(8,128)S(1)}, u32[]{:S(2)}, u32[]{:S(2)}) async-start(f32[8,72,128]{2,1,0:T(8,128)} %shard_map.61), calls=%async_computation.1 | async-start | bytes 589824 | tf_op jit(solution)/shard_map/all_to_all | solution.py:137
  39.0 9.3 %all-to-all-done.1.parts_ref = f32[8,72,128]{2,1,0:T(8,128)S(1)} async-done(((f32[8,72,128]{2,1,0:T(8,128)}), f32[8,72,128]{2,1,0:T(8,128)S(1)}, u32[]{:S(2)}, u32[]{:S(2)}) %all-to-all-start.1) | async-done | bytes 294944 | tf_op jit(solution)/shard_map/all_to_all | solution.py:137
  48.3 0.0 copy-done
  48.3 0.0 copy-done.1
  48.3 12.3 %shard_map.62 = (f32[32,128]{1,0:T(8,128)}, bf16[32,128]{1,0:T(8,128)(2,1)S(1)}) custom-call(s32[1]{0:T(128)S(6)} %copy.20.rank_ref, f32[8,72,128]{2,1,0:T(8,128)S(1)} %all-to-all-done.1.parts_ref, f32[1,128]{1,0:T(1,128)S(1)} %bitcast.16, f32[32,128]{1,0:T(8,128)S(1)} %bitcast.15), custom_call_target="tpu_custom_call" | custom-call | tf_op jit(solution)/shard_map/pallas_call | solution.py:138
  60.7 4.8 %fusion.4 = bf16[4,8,128,128]{3,1,2,0:T(8,128)(2,1)S(1)} fusion(bf16[32,128]{1,0:T(8,128)(2,1)S(1)} %get-tuple-element.4, bf16[16,8,128,128]{3,2,1,0:T(8,128)(2,1)} %bitcast.17), kind=kOutput, calls=%fused_computation.5 | convolution fusion | flops 134742016 | bytes 5251072 | tf_op jit(solution)/shard_map/dot_general | solution.py:149
  65.5 1.2 %copy.9 = bf16[4,8,128,128]{3,2,1,0:T(8,128)(2,1)} copy(bf16[4,8,128,128]{3,1,2,0:T(8,128)(2,1)S(1)} %fusion.4) | data formatting | bytes 2097152
  (1 shorter events, 0.0 us)
Async XLA Ops:
  0.6 47.7 %copy-start = (f32[128,32]{0,1:T(8,128)S(1)}, f32[128,32]{0,1:T(8,128)}, u32[]{:S(2)}) copy-start(f32[128,32]{0,1:T(8,128)} %param.6) | copy-start | bytes 49156
  0.6 47.7 %copy-start.1 = (f32[128]{0:T(128)S(1)}, f32[128]{0:T(128)}, u32[]{:S(2)}) copy-start(f32[128]{0:T(128)} %param.5) | copy-start | bytes 1540
  8.9 4.2 %collective-permute-start = (f32[72,128]{1,0:T(8,128)S(1)}, f32[72,128]{1,0:T(8,128)S(1)}, u32[]{:S(2)}, u32[]{:S(2)}) collective-permute-start(f32[72,128]{1,0:T(8,128)S(1)} %shard_map.59.a_ref), channel_id=1, source_target_pairs={{0,1},{1,0},{2,3},{3,2},{4,5},{5,4},{6,7},{7,6},{8,9},{9,8},{10,11... | collective-permute-start | bytes 110600 | tf_op jit(solution)/shard_map/ppermute | solution.py:128
  30.1 18.2 %all-to-all-start.1 = ((f32[8,72,128]{2,1,0:T(8,128)}), f32[8,72,128]{2,1,0:T(8,128)S(1)}, u32[]{:S(2)}, u32[]{:S(2)}) async-start(f32[8,72,128]{2,1,0:T(8,128)} %shard_map.61), calls=%async_computation.1 | async-start | bytes 589824 | tf_op jit(solution)/shard_map/all_to_all | solution.py:137

commit v2 on v0

v2 whole, which is shorter than its diff:
```python
import functools

import jax
import jax.numpy as jnp
from jax import lax
from jax.experimental import pallas as pl
from jax.experimental.pallas import tpu as pltpu
from jax.sharding import PartitionSpec as P

ITERS = 4
ROWS = 16
VMEM = pl.BlockSpec(memory_space=pltpu.VMEM)
SMEM = pl.BlockSpec(memory_space=pltpu.SMEM)
ANY = pl.BlockSpec(memory_space=pl.ANY)
SMALL = pltpu.CompilerParams(vmem_limit_bytes=4 * 2**20)
MOST = pltpu.CompilerParams(vmem_limit_bytes=50 * 2**20)
LARGE = pltpu.CompilerParams(vmem_limit_bytes=16 * 2**20)


def iota(shape, dim):
    return lax.broadcasted_iota(jnp.int32, shape, dim)


def f32(*shape):
    return jax.ShapeDtypeStruct(shape, jnp.float32)


def split3(x):
    a = x.astype(jnp.bfloat16)
    rest = x - a.astype(jnp.float32)
    b = rest.astype(jnp.bfloat16)
    c = (rest - b.astype(jnp.float32)).astype(jnp.bfloat16)
    return a, b, c


def fetch(data_ref, held_ref, sem):
    return [
        pltpu.make_async_copy(
            data_ref.at[:, pl.ds(ROWS * n, ROWS), :], held_ref.at[n], sem.at[n]
        )
        for n in range(held_ref.shape[0])
    ]


def columns_of(block):
    t = jnp.swapaxes(block, 0, 1)
    return jnp.concatenate([t[i] for i in range(t.shape[0])], axis=1)


def gram_kernel(data_ref, mine_ref, theirs_ref, held_ref, sem, *, axis):
    copies = fetch(data_ref, held_ref, sem)
    for copy in copies:
        copy.start()
    v = held_ref.shape[1]
    h = v // 2
    gram = jnp.zeros((v, v), jnp.float32)
    for n, copy in enumerate(copies):
        copy.wait()
        x = columns_of(held_ref[n])
        gram = gram + lax.dot_general(x, x, (((1,), (1,)), ((), ())), preferred_element_type=jnp.float32)
    lower_right = pltpu.roll(gram[h:], h, 1)
    row, col = iota((h, v), 0), iota((h, v), 1)
    top = jnp.where((col >= h) | (row >= col), gram[:h], lower_right)
    diagonal = jnp.sum(jnp.where(iota((v, v), 0) == iota((v, v), 1), gram, 0.0), axis=0, keepdims=True)
    lower = lax.rem(lax.axis_index(axis), 2) == 0
    first, second = top[: h // 2], top[h // 2 :]
    mine_ref[: h // 2] = jnp.where(lower, first, second)
    theirs_ref[: h // 2] = jnp.where(lower, second, first)
    diagonal = jnp.broadcast_to(diagonal, (mine_ref.shape[0] - h // 2, v))
    mine_ref[h // 2 :] = diagonal
    theirs_ref[h // 2 :] = diagonal


def unpack(first, second, v):
    h = v // 2
    q = jnp.concatenate([first[: h // 2], second[: h // 2]] * 2, axis=0)
    qt = q.T
    row, col = iota((v, v), 0), iota((v, v), 1)
    top = jnp.where((col >= h) | (row >= col), q, qt)
    shifted = pltpu.roll(q, h, 1)
    shifted_t = jnp.concatenate([qt[h:], qt[:h]], axis=0)
    corner = jnp.where(row < col, shifted, shifted_t)
    corner = jnp.where(row == col, first[h // 2 : h // 2 + 1], corner)
    bottom = jnp.where(col < h, qt, corner)
    return jnp.where(row < h, top, bottom)


def pair_kernel(mine_ref, theirs_ref, out_ref):
    total = mine_ref[...] + theirs_ref[...]
    for n in range(out_ref.shape[0]):
        out_ref[n] = total


def total_of(ref):
    total = ref[0]
    for n in range(1, ref.shape[0]):
        total = total + ref[n]
    return total


def many_kernel(in_ref, out_ref):
    total = total_of(in_ref)
    for n in range(out_ref.shape[0]):
        out_ref[n] = total


def sum_kernel(in_ref, out_ref):
    out_ref[...] = total_of(in_ref)


def eliminate(inner, image, out_ref, beside):
    n, v = image.shape
    blocks = n // 8
    a = [inner[8 * c : 8 * c + 8] for c in range(blocks)]
    y = [image[8 * c : 8 * c + 8] for c in range(blocks)]

    def full(x):
        return jnp.broadcast_to(x, (8, v))

    for b in range(blocks):
        beside(b)
        rows_a = [jnp.broadcast_to(a[b][t : t + 1], (8, n)) for t in range(8)]
        rows_y = [full(y[b][t : t + 1]) for t in range(8)]
        cols = {c: [full(a[c][:, 8 * b + t : 8 * b + t + 1]) for t in range(8)] for c in range(b + 1, blocks)}
        p = [[full(a[b][t : t + 1, 8 * b + u : 8 * b + u + 1]) for u in range(t + 1)] for t in range(8)]
        for u in range(8):
            r = lax.rsqrt(p[u][u])
            low = {t: p[t][u] * r for t in range(u + 1, 8)}
            for t in low:
                for x in range(u + 1, t + 1):
                    p[t][x] = p[t][x] - low[t] * low[x]
            rows_a[u] = rows_a[u] * r[:, :n]
            rows_y[u] = rows_y[u] * r
            for c in cols:
                cols[c][u] = cols[c][u] * r
            for t in low:
                rows_a[t] = rows_a[t] - low[t][:, :n] * rows_a[u]
                rows_y[t] = rows_y[t] - low[t] * rows_y[u]
                for c in cols:
                    cols[c][t] = cols[c][t] - low[t] * cols[c][u]
            out_ref[8 * b + u : 8 * b + u + 1, :] = rows_y[u][:1]
        for c in cols:
            for u in range(8):
                a[c] = a[c] - cols[c][u][:, :n] * rows_a[u]
                y[c] = y[c] - cols[c][u] * rows_y[u]


def final_kernel(
    rank_ref, mine_ref, theirs_ref, scale_ref, start_ref, data_ref, factor_ref, core_ref,
    turned_ref, held_ref, g_ref, basis_ref, sem, *, axis
):
    v = scale_ref.shape[1]
    pieces = held_ref.shape[0]
    blocks = start_ref.shape[0] // 8

    def turn_data(turn, b):
        shares = ITERS * blocks
        first, last = ((turn * blocks + b + end) * pieces * 2 // shares for end in (0, 1))
        for n in range(first, last):
            piece, half = divmod(n, 2)
            some = slice(half * (v // 2), (half + 1) * (v // 2))
            rows = slice(piece * ROWS, (piece + 1) * ROWS)
            turned_ref[piece, :, some, :] = jnp.swapaxes(data_ref[some, rows, :], 0, 1)

    lower = lax.rem(lax.axis_index(axis), 2) == 0
    mine, theirs = mine_ref[...], theirs_ref[...]
    g1, g2, g3 = split3(unpack(jnp.where(lower, mine, theirs), jnp.where(lower, theirs, mine), v))
    for n, piece in enumerate((g1, g2, g1, g3, g2, g1)):
        g_ref[n * v : (n + 1) * v] = piece
    scale = scale_ref[...]
    basis = start_ref[...]
    for turn in range(ITERS):
        x1, x2, x3 = split3(basis * scale)
        x = jnp.concatenate([x1, x1, x2, x1, x2, x3], axis=1)
        image = jnp.dot(x, g_ref[...], preferred_element_type=jnp.float32) * scale
        y1, y2, y3 = split3(image)
        left = jnp.concatenate([y1, y1, y2, y1, y2, y3], axis=1)
        right = jnp.concatenate([y1, y2, y1, y3, y2, y1], axis=1)
        inner = lax.dot_general(left, right, (((1,), (1,)), ((), ())), preferred_element_type=jnp.float32)
        eliminate(inner, image, basis_ref, functools.partial(turn_data, turn))
        basis = basis_ref[...]
    factor = jnp.where(iota(basis.shape, 0) < rank_ref[0], basis, 0.0)
    factor_ref[...] = factor
    scaled = (factor * scale).astype(jnp.bfloat16)
    outs = []
    for n in range(pieces):
        product = [
            jnp.dot(scaled, turned_ref[n, i], preferred_element_type=jnp.float32).astype(jnp.bfloat16)
            for i in range(ROWS)
        ]
        held_ref[n] = jnp.swapaxes(jnp.stack(product), 0, 1)
        outs.append(
            pltpu.make_async_copy(held_ref.at[n], core_ref.at[:, pl.ds(ROWS * n, ROWS), :], sem.at[n])
        )
        outs[-1].start()
    for copy in outs:
        copy.wait()


def gram_call(data, axis="gy"):
    variables, rows, cells = data.shape
    pieces = rows // ROWS
    return pl.pallas_call(
        functools.partial(gram_kernel, axis=axis),
        out_shape=(f32(variables // 4 + 8, variables),) * 2,
        in_specs=[ANY],
        out_specs=(VMEM, VMEM),
        compiler_params=MOST,
        scratch_shapes=[
            pltpu.VMEM((pieces, variables, ROWS, cells), jnp.bfloat16),
            pltpu.SemaphoreType.DMA((pieces,)),
        ],
    )(data)


def final_call(rank, mine, theirs, inv_scale, start, data, axis="gy"):
    variables, rows, cells = data.shape
    columns = start.shape[1]
    pieces = rows // ROWS
    return pl.pallas_call(
        functools.partial(final_kernel, axis=axis),
        out_shape=(f32(columns, variables), jax.ShapeDtypeStruct((columns, rows, cells), jnp.bfloat16)),
        in_specs=[SMEM, VMEM, VMEM, VMEM, VMEM, VMEM],
        out_specs=(VMEM, ANY),
        compiler_params=LARGE,
        scratch_shapes=[
            pltpu.VMEM((pieces, ROWS, variables, cells), jnp.bfloat16),
            pltpu.VMEM((pieces, columns, ROWS, cells), jnp.bfloat16),
            pltpu.VMEM((6 * variables, variables), jnp.bfloat16),
            pltpu.VMEM((columns, variables), jnp.float32),
            pltpu.SemaphoreType.DMA((pieces,)),
        ],
    )(rank, mine, theirs, inv_scale[None, :], start.T, data)


def call(kernel, shape, *args):
    return pl.pallas_call(
        kernel, out_shape=f32(*shape), in_specs=[VMEM] * len(args), out_specs=VMEM, compiler_params=SMALL
    )(*args)


def body(data, inv_scale, start, rank):
    variables = data.shape[0]
    nx, ny = lax.axis_size("gx"), lax.axis_size("gy")
    swap = [(i, i ^ 1) for i in range(ny)]
    cores = [[2 * i + c for i in range(ny // 2)] for c in range(2)]
    mine, theirs = gram_call(data)
    theirs = lax.ppermute(theirs, "gy", swap)
    piece = mine.shape
    got = lax.all_to_all(
        call(pair_kernel, (ny // 2, *piece), mine, theirs), "gy", 0, 0, axis_index_groups=cores
    )
    got = lax.all_to_all(call(many_kernel, (nx, *piece), got), "gx", 0, 0)
    mine = call(sum_kernel, piece, got)
    theirs = lax.ppermute(mine, "gy", swap)
    factor_t, core = final_call(rank, mine, theirs, inv_scale, start, data)
    return (core, factor_t.T)


def solution(mesh):
    in_specs = (P(None, "gx", "gy"), P(), P(), P())
    out_specs = (P(None, "gx", "gy"), P())
    return jax.shard_map(body, mesh=mesh, in_specs=in_specs, out_specs=out_specs, check_vma=False)
```

time: 304 us -> 51.6 us (0.17)
  waiting for transfers between devices: 241 us -> 1.04 us
  blocking collectives: 0 us -> 29.2 us
  other arithmetic: 26.8 us -> 0 us
  matrix products: 19.6 us -> 0 us
  between operations: 14.9 us -> 1.33 us
  Pallas kernels: 0 us -> 13 us
  starting transfers between devices: 0.04 us -> 6.89 us
    psum x1 -> x0, waiting for transfers between devices: 241 us -> none  [body(): gram = lax.psum(local_gram, ('gx', 'gy'))]
    all_to_all x0 -> x2, blocking collectives: none -> 29.2 us  [the longest x1 16.4 us: body(): got = lax.all_to_all(call(many_kernel, (nx, *piece), got), 'gx', 0, 0)]
    another operation x20 -> x0, other arithmetic: 26.7 us -> none  [the longest x12 14.4 us: body(): lower = jnp.linalg.cholesky(inner)]
    dot_general x10 -> x0, matrix products: 18.7 us -> none  [the longest x1 8.76 us: body(): lax.dot_general(flat, flat, (((1,), (1,)), ((), ())), preferred_element_t...]
    pallas_call x0 -> x5, Pallas kernels: none -> 13 us  [the longest x1 8.58 us: final_call(): pl.pallas_call(functools.partial(final_kernel, axis=axis), out_shape=(f32...]
    ppermute x0 -> x2, starting transfers between devices: none -> 6.89 us  [the longest x1 3.56 us: body(): theirs = lax.ppermute(mine, 'gy', swap)]
  transfers between devices with their start and end apart: 1 -> 2, of which waited for: 1 -> 2; matrix products, arithmetic and copies ran while one was open for 0% -> 0% of each run, Pallas kernels for 0% -> 0%
where the time goes in v2:
time: 51.6 us; the launch traced here: 51.4 us
  blocking collectives  29.2 us (57%)
  Pallas kernels  13 us (25%)
  starting transfers between devices  6.89 us (13%)
  between operations  1.33 us (3%)
  waiting for transfers between devices  1.04 us (2%)
    all_to_all x1, blocking collectives, body(): got = lax.all_to_all(call(many_kernel, (nx, *piece), got), 'gx', 0, 0)  16.4 us
    all_to_all x1, blocking collectives, body(): lax.all_to_all(call(pair_kernel, (ny // 2, *piece), mine, theirs), 'gy',...  12.8 us
    pallas_call x1, Pallas kernels, final_call(): pl.pallas_call(functools.partial(final_kernel, axis=axis), out_shape=(f32...  8.58 us
    pallas_call x1, Pallas kernels, gram_call(): pl.pallas_call(functools.partial(gram_kernel, axis=axis), out_shape=(f32(...  4.31 us
    ppermute x1, starting transfers between devices, body(): theirs = lax.ppermute(mine, 'gy', swap)  3.56 us
    ppermute x1, starting transfers between devices, body(): theirs = lax.ppermute(theirs, 'gy', swap)  3.33 us
  transfers between devices with their start and end apart: 2, of which 2 were waited for; matrix products, arithmetic and copies ran while one was open for 0% of the time, Pallas kernels for 0%

profile of v2, /device:TPU:1, one launch (start us, length us, event | category | flops | bytes accessed | tf_op | source)
XLA Modules:
  0.0 51.4 jit_solution(6811675484923815717)
XLA Ops:
  0.6 0.0 copy-start
  0.6 0.0 copy-start.1
  0.6 0.0 copy-start.2
  0.7 4.3 %shard_map.59 = (f32[40,128]{1,0:T(8,128)S(1)}, f32[40,128]{1,0:T(8,128)S(1)}) custom-call(bf16[128,128,128]{2,1,0:T(8,128)(2,1)} %data_ref.3), custom_call_target="tpu_custom_call" | custom-call | tf_op jit(solution)/shard_map/pallas_call | solution.py:203
  5.0 3.3 %collective-permute-start = (f32[40,128]{1,0:T(8,128)S(1)}, f32[40,128]{1,0:T(8,128)S(1)}, u32[]{:S(2)}, u32[]{:S(2)}) collective-permute-start(f32[40,128]{1,0:T(8,128)S(1)} %get-tuple-element.7), channel_id=1, source_target_pairs={{0,1},{1,0},{2,3},{3,2},{4,5},{5,4},{6,7},{7,6},{8,9},{9,8},{10,11... | collective-permute-start | bytes 61448 | tf_op jit(solution)/shard_map/ppermute | solution.py:248
  8.3 0.8 %collective-permute-done.theirs_ref = f32[40,128]{1,0:T(8,128)S(1)} collective-permute-done((f32[40,128]{1,0:T(8,128)S(1)}, f32[40,128]{1,0:T(8,128)S(1)}, u32[]{:S(2)}, u32[]{:S(2)}) %collective-permute-start) | collective-permute-done | bytes 20512 | tf_op jit(solution)/shard_map/ppermute | solution.py:248
  9.2 12.8 %all_to_all.10.in_ref = f32[16,40,128]{2,1,0:T(8,128)S(1)} all-to-all(f32[16,40,128]{2,1,0:T(8,128)S(1)} %shard_map.60), channel_id=1, replica_groups={{0,2,4,6,8,10,12,14,16,18,20,22,24,26,28,30},{1,3,5,7,9,11,13,15,17,19,..., dimensions={0} | all-to-all | bytes 655360 | tf_op jit(solution)/shard_map/all_to_all | solution.py:250
  22.0 16.4 %all_to_all.11.in_ref = f32[8,40,128]{2,1,0:T(8,128)S(1)} all-to-all(f32[8,40,128]{2,1,0:T(8,128)S(1)} %shard_map.61), channel_id=1, replica_groups=mesh['gx'=8,'gy'=32] {'gx'}, dimensions={0} | all-to-all | bytes 327680 | tf_op jit(solution)/shard_map/all_to_all | solution.py:253
  38.4 3.6 %collective-permute-start.1 = (f32[40,128]{1,0:T(8,128)S(1)}, f32[40,128]{1,0:T(8,128)S(1)}, u32[]{:S(2)}, u32[]{:S(2)}) collective-permute-start(f32[40,128]{1,0:T(8,128)S(1)} %shard_map.62.mine_ref), channel_id=1, source_target_pairs={{0,1},{1,0},{2,3},{3,2},{4,5},{5,4},{6,7},{7,6},{8,9},{9,8},{10,11... | collective-permute-start | bytes 61448 | tf_op jit(solution)/shard_map/ppermute | solution.py:255
  42.6 0.2 collective-permute-done.1.theirs_ref
  42.8 0.0 copy-done
  42.8 0.0 copy-done.1
  42.8 0.0 copy-done.2
  42.8 8.6 %shard_map.63 = (f32[32,128]{1,0:T(8,128)}, bf16[32,128,128]{2,1,0:T(8,128)(2,1)}) custom-call(s32[1]{0:T(128)S(6)} %copy.6.rank_ref, f32[40,128]{1,0:T(8,128)S(1)} %shard_map.62.mine_ref, f32[40,128]{1,0:T(8,128)S(1)} %collective-permute-done.1.theirs_ref, f32[1,128]{1,0:T(1,128)S(1)} %bitcast.4, f32[32,128]{1,0:T(8,128)S(1)} %bitcast.3, ...), custom_call_target="tpu_custom_call" | custom-call | tf_op jit(solution)/shard_map/pallas_call | solution.py:220
  (3 shorter events, 0.1 us)
Async XLA Ops:
  0.6 42.2 %copy-start = (bf16[128,128,128]{2,1,0:T(8,128)(2,1)S(1)}, bf16[128,128,128]{2,1,0:T(8,128)(2,1)}, u32[]{:S(2)}) copy-start(bf16[128,128,128]{2,1,0:T(8,128)(2,1)} %data_ref.3) | copy-start | bytes 12582916
  0.6 42.2 %copy-start.1 = (f32[128,32]{0,1:T(8,128)S(1)}, f32[128,32]{0,1:T(8,128)}, u32[]{:S(2)}) copy-start(f32[128,32]{0,1:T(8,128)} %param.6) | copy-start | bytes 49156
  0.6 42.1 %copy-start.2 = (f32[128]{0:T(128)S(1)}, f32[128]{0:T(128)}, u32[]{:S(2)}) copy-start(f32[128]{0:T(128)} %param.5) | copy-start | bytes 1540
  5.0 4.2 %collective-permute-start = (f32[40,128]{1,0:T(8,128)S(1)}, f32[40,128]{1,0:T(8,128)S(1)}, u32[]{:S(2)}, u32[]{:S(2)}) collective-permute-start(f32[40,128]{1,0:T(8,128)S(1)} %get-tuple-element.7), channel_id=1, source_target_pairs={{0,1},{1,0},{2,3},{3,2},{4,5},{5,4},{6,7},{7,6},{8,9},{9,8},{10,11... | collective-permute-start | bytes 61448 | tf_op jit(solution)/shard_map/ppermute | solution.py:248
  38.4 4.4 %collective-permute-start.1 = (f32[40,128]{1,0:T(8,128)S(1)}, f32[40,128]{1,0:T(8,128)S(1)}, u32[]{:S(2)}, u32[]{:S(2)}) collective-permute-start(f32[40,128]{1,0:T(8,128)S(1)} %shard_map.62.mine_ref), channel_id=1, source_target_pairs={{0,1},{1,0},{2,3},{3,2},{4,5},{5,4},{6,7},{7,6},{8,9},{9,8},{10,11... | collective-permute-start | bytes 61448 | tf_op jit(solution)/shard_map/ppermute | solution.py:255

commit v3 on v2

--- a/solution.py
+++ b/solution.py
@@ -86,7 +86,8 @@
 
 
 def pair_kernel(mine_ref, theirs_ref, out_ref):
-    total = mine_ref[...] + theirs_ref[...]
+    count, lines, v = out_ref.shape[1:]
+    total = (mine_ref[...] + theirs_ref[...])[: count * lines].reshape(count, lines, v)
     for n in range(out_ref.shape[0]):
         out_ref[n] = total
 
@@ -105,7 +106,10 @@
 
 
 def sum_kernel(in_ref, out_ref):
-    out_ref[...] = total_of(in_ref)
+    total = total_of(in_ref)
+    rows = total.shape[0] * total.shape[1]
+    out_ref[:rows] = total.reshape(rows, total.shape[2])
+    out_ref[rows:] = jnp.zeros((out_ref.shape[0] - rows, out_ref.shape[1]), jnp.float32)
 
 
 def eliminate(inner, image, out_ref, beside):
@@ -122,7 +126,8 @@
         rows_a = [jnp.broadcast_to(a[b][t : t + 1], (8, n)) for t in range(8)]
         rows_y = [full(y[b][t : t + 1]) for t in range(8)]
         cols = {c: [full(a[c][:, 8 * b + t : 8 * b + t + 1]) for t in range(8)] for c in range(b + 1, blocks)}
-        p = [[full(a[b][t : t + 1, 8 * b + u : 8 * b + u + 1]) for u in range(t + 1)] for t in range(8)]
+        pivot = [full(a[b][:, 8 * b + u : 8 * b + u + 1]) for u in range(8)]
+        p = [[full(pivot[u][t : t + 1]) for u in range(t + 1)] for t in range(8)]
         for u in range(8):
             r = lax.rsqrt(p[u][u])
             low = {t: p[t][u] * r for t in range(u + 1, 8)}
@@ -168,17 +173,22 @@
     for n, piece in enumerate((g1, g2, g1, g3, g2, g1)):
         g_ref[n * v : (n + 1) * v] = piece
     scale = scale_ref[...]
-    basis = start_ref[...]
+
+    def weigh(x):
+        x1, x2, x3 = split3(x * scale)
+        x = jnp.concatenate([x1, x1, x2, x1, x2, x3], axis=1)
+        return jnp.dot(x, g_ref[...], preferred_element_type=jnp.float32) * scale
+
+    image = weigh(start_ref[...])
     for turn in range(ITERS):
-        x1, x2, x3 = split3(basis * scale)
-        x = jnp.concatenate([x1, x1, x2, x1, x2, x3], axis=1)
-        image = jnp.dot(x, g_ref[...], preferred_element_type=jnp.float32) * scale
         y1, y2, y3 = split3(image)
         left = jnp.concatenate([y1, y1, y2, y1, y2, y3], axis=1)
         right = jnp.concatenate([y1, y2, y1, y3, y2, y1], axis=1)
         inner = lax.dot_general(left, right, (((1,), (1,)), ((), ())), preferred_element_type=jnp.float32)
-        eliminate(inner, image, basis_ref, functools.partial(turn_data, turn))
-        basis = basis_ref[...]
+        solved = weigh(image) if turn < ITERS - 1 else image
+        eliminate(inner, solved, basis_ref, functools.partial(turn_data, turn))
+        image = basis_ref[...]
+    basis = image
     factor = jnp.where(iota(basis.shape, 0) < rank_ref[0], basis, 0.0)
     factor_ref[...] = factor
     scaled = (factor * scale).astype(jnp.bfloat16)
@@ -246,12 +256,12 @@
     cores = [[2 * i + c for i in range(ny // 2)] for c in range(2)]
     mine, theirs = gram_call(data)
     theirs = lax.ppermute(theirs, "gy", swap)
-    piece = mine.shape
+    piece = (variables // 16 + 1, 4, variables)
     got = lax.all_to_all(
         call(pair_kernel, (ny // 2, *piece), mine, theirs), "gy", 0, 0, axis_index_groups=cores
     )
     got = lax.all_to_all(call(many_kernel, (nx, *piece), got), "gx", 0, 0)
-    mine = call(sum_kernel, piece, got)
+    mine = call(sum_kernel, theirs.shape, got)
     theirs = lax.ppermute(mine, "gy", swap)
     factor_t, core = final_call(rank, mine, theirs, inv_scale, start, data)
     return (core, factor_t.T)

time: 51.6 us -> 50.7 us (0.983)
  no operation moved by 1% of the time
where the time goes in v3:
time: 50.7 us; the launch traced here: 50.5 us
  blocking collectives  28.8 us (57%)
  Pallas kernels  12.6 us (25%)
  starting transfers between devices  6.77 us (13%)
  between operations  1.33 us (3%)
  waiting for transfers between devices  1.04 us (2%)
    all_to_all x1, blocking collectives, body(): got = lax.all_to_all(call(many_kernel, (nx, *piece), got), 'gx', 0, 0)  16.2 us
    all_to_all x1, blocking collectives, body(): lax.all_to_all(call(pair_kernel, (ny // 2, *piece), mine, theirs), 'gy',...  12.6 us
    pallas_call x1, Pallas kernels, final_call(): pl.pallas_call(functools.partial(final_kernel, axis=axis), out_shape=(f32...  8.21 us
    pallas_call x1, Pallas kernels, gram_call(): pl.pallas_call(functools.partial(gram_kernel, axis=axis), out_shape=(f32(...  4.31 us
    ppermute x1, starting transfers between devices, body(): theirs = lax.ppermute(mine, 'gy', swap)  3.44 us
    ppermute x1, starting transfers between devices, body(): theirs = lax.ppermute(theirs, 'gy', swap)  3.33 us
  transfers between devices with their start and end apart: 2, of which 2 were waited for; matrix products, arithmetic and copies ran while one was open for 0% of the time, Pallas kernels for 0%

profile of v3, /device:TPU:1, one launch (start us, length us, event | category | flops | bytes accessed | tf_op | source)
XLA Modules:
  0.0 50.5 jit_solution(8984380398655719895)
XLA Ops:
  0.6 0.0 copy-start
  0.6 0.0 copy-start.1
  0.6 0.0 copy-start.2
  0.7 4.3 %shard_map.59 = (f32[40,128]{1,0:T(8,128)S(1)}, f32[40,128]{1,0:T(8,128)S(1)}) custom-call(bf16[128,128,128]{2,1,0:T(8,128)(2,1)} %data_ref.3), custom_call_target="tpu_custom_call" | custom-call | tf_op jit(solution)/shard_map/pallas_call | solution.py:213
  5.0 3.3 %collective-permute-start = (f32[40,128]{1,0:T(8,128)S(1)}, f32[40,128]{1,0:T(8,128)S(1)}, u32[]{:S(2)}, u32[]{:S(2)}) collective-permute-start(f32[40,128]{1,0:T(8,128)S(1)} %get-tuple-element.7), channel_id=1, source_target_pairs={{0,1},{1,0},{2,3},{3,2},{4,5},{5,4},{6,7},{7,6},{8,9},{9,8},{10,11... | collective-permute-start | bytes 61448 | tf_op jit(solution)/shard_map/ppermute | solution.py:258
  8.3 0.8 %collective-permute-done.theirs_ref = f32[40,128]{1,0:T(8,128)S(1)} collective-permute-done((f32[40,128]{1,0:T(8,128)S(1)}, f32[40,128]{1,0:T(8,128)S(1)}, u32[]{:S(2)}, u32[]{:S(2)}) %collective-permute-start) | collective-permute-done | bytes 20512 | tf_op jit(solution)/shard_map/ppermute | solution.py:258
  9.2 12.6 %all_to_all.10.in_ref = f32[16,9,4,128]{3,2,1,0:T(4,128)S(1)} all-to-all(f32[16,9,4,128]{3,2,1,0:T(4,128)S(1)} %shard_map.60), channel_id=1, replica_groups={{0,2,4,6,8,10,12,14,16,18,20,22,24,26,28,30},{1,3,5,7,9,11,13,15,17,19,..., dimensions={0} | all-to-all | bytes 589824 | tf_op jit(solution)/shard_map/all_to_all | solution.py:260
  21.8 16.2 %all_to_all.11.in_ref = f32[8,9,4,128]{3,2,1,0:T(4,128)S(1)} all-to-all(f32[8,9,4,128]{3,2,1,0:T(4,128)S(1)} %shard_map.61), channel_id=1, replica_groups=mesh['gx'=8,'gy'=32] {'gx'}, dimensions={0} | all-to-all | bytes 294912 | tf_op jit(solution)/shard_map/all_to_all | solution.py:263
  38.0 3.4 %collective-permute-start.1 = (f32[40,128]{1,0:T(8,128)S(1)}, f32[40,128]{1,0:T(8,128)S(1)}, u32[]{:S(2)}, u32[]{:S(2)}) collective-permute-start(f32[40,128]{1,0:T(8,128)S(1)} %shard_map.62.mine_ref), channel_id=1, source_target_pairs={{0,1},{1,0},{2,3},{3,2},{4,5},{5,4},{6,7},{7,6},{8,9},{9,8},{10,11... | collective-permute-start | bytes 61448 | tf_op jit(solution)/shard_map/ppermute | solution.py:265
  42.1 0.2 collective-permute-done.1.theirs_ref
  42.3 0.0 copy-done
  42.3 0.0 copy-done.1
  42.3 0.0 copy-done.2
  42.3 8.2 %shard_map.63 = (f32[32,128]{1,0:T(8,128)}, bf16[32,128,128]{2,1,0:T(8,128)(2,1)}) custom-call(s32[1]{0:T(128)S(6)} %copy.6.rank_ref, f32[40,128]{1,0:T(8,128)S(1)} %shard_map.62.mine_ref, f32[40,128]{1,0:T(8,128)S(1)} %collective-permute-done.1.theirs_ref, f32[1,128]{1,0:T(1,128)S(1)} %bitcast.4, f32[32,128]{1,0:T(8,128)S(1)} %bitcast.3, ...), custom_call_target="tpu_custom_call" | custom-call | tf_op jit(solution)/shard_map/pallas_call | solution.py:230
  (3 shorter events, 0.1 us)
Async XLA Ops:
  0.6 41.7 %copy-start = (bf16[128,128,128]{2,1,0:T(8,128)(2,1)S(1)}, bf16[128,128,128]{2,1,0:T(8,128)(2,1)}, u32[]{:S(2)}) copy-start(bf16[128,128,128]{2,1,0:T(8,128)(2,1)} %data_ref.3) | copy-start | bytes 12582916
  0.6 41.7 %copy-start.1 = (f32[128,32]{0,1:T(8,128)S(1)}, f32[128,32]{0,1:T(8,128)}, u32[]{:S(2)}) copy-start(f32[128,32]{0,1:T(8,128)} %param.6) | copy-start | bytes 49156
  0.6 41.7 %copy-start.2 = (f32[128]{0:T(128)S(1)}, f32[128]{0:T(128)}, u32[]{:S(2)}) copy-start(f32[128]{0:T(128)} %param.5) | copy-start | bytes 1540
  5.0 4.2 %collective-permute-start = (f32[40,128]{1,0:T(8,128)S(1)}, f32[40,128]{1,0:T(8,128)S(1)}, u32[]{:S(2)}, u32[]{:S(2)}) collective-permute-start(f32[40,128]{1,0:T(8,128)S(1)} %get-tuple-element.7), channel_id=1, source_target_pairs={{0,1},{1,0},{2,3},{3,2},{4,5},{5,4},{6,7},{7,6},{8,9},{9,8},{10,11... | collective-permute-start | bytes 61448 | tf_op jit(solution)/shard_map/ppermute | solution.py:258
  38.0 4.3 %collective-permute-start.1 = (f32[40,128]{1,0:T(8,128)S(1)}, f32[40,128]{1,0:T(8,128)S(1)}, u32[]{:S(2)}, u32[]{:S(2)}) collective-permute-start(f32[40,128]{1,0:T(8,128)S(1)} %shard_map.62.mine_ref), channel_id=1, source_target_pairs={{0,1},{1,0},{2,3},{3,2},{4,5},{5,4},{6,7},{7,6},{8,9},{9,8},{10,11... | collective-permute-start | bytes 61448 | tf_op jit(solution)/shard_map/ppermute | solution.py:265

commit v4 on v3

--- a/solution.py
+++ b/solution.py
@@ -99,10 +99,11 @@
     return total
 
 
-def many_kernel(in_ref, out_ref):
-    total = total_of(in_ref)
-    for n in range(out_ref.shape[0]):
-        out_ref[n] = total
+def add_kernel(*refs):
+    total = refs[0][...]
+    for ref in refs[1:-1]:
+        total = total + ref[...]
+    refs[-1][...] = total
 
 
 def sum_kernel(in_ref, out_ref):
@@ -257,10 +258,13 @@
     mine, theirs = gram_call(data)
     theirs = lax.ppermute(theirs, "gy", swap)
     piece = (variables // 16 + 1, 4, variables)
+    mine = call(add_kernel, mine.shape, mine, theirs)
+    theirs = [lax.ppermute(mine, "gx", [(n, n ^ d) for n in range(nx)]) for d in (1, 2, 3)]
+    mine = call(add_kernel, mine.shape, mine, *theirs)
+    theirs = lax.ppermute(mine, "gx", [(n, n ^ (nx // 2)) for n in range(nx)])
     got = lax.all_to_all(
         call(pair_kernel, (ny // 2, *piece), mine, theirs), "gy", 0, 0, axis_index_groups=cores
     )
-    got = lax.all_to_all(call(many_kernel, (nx, *piece), got), "gx", 0, 0)
     mine = call(sum_kernel, theirs.shape, got)
     theirs = lax.ppermute(mine, "gy", swap)
     factor_t, core = final_call(rank, mine, theirs, inv_scale, start, data)

time: 50.7 us -> 49.7 us (0.980)
  blocking collectives: 28.8 us -> 14.1 us
  starting transfers between devices: 6.77 us -> 16 us
  waiting for transfers between devices: 1.04 us -> 5.61 us
    all_to_all x1 -> x0, blocking collectives: 16.2 us -> none  [body(): got = lax.all_to_all(call(many_kernel, (nx, *piece), got), 'gx', 0, 0)]
    ppermute x0 -> x4, starting transfers between devices: none -> 8.2 us  [the longest x1 4.65 us: body(): theirs = lax.ppermute(mine, 'gx', [(n, n ^ nx // 2) for n in range(nx)])]
    ppermute x0 -> x4, waiting for transfers between devices: none -> 4.57 us  [the longest x3 2.59 us: body(): lax.ppermute(mine, 'gx', [(n, n ^ d) for n in range(nx)])]
    all_to_all x1, blocking collectives: 12.6 us -> 14.1 us  [body(): lax.all_to_all(call(pair_kernel, (ny // 2, *piece), mine, theirs), 'gy',...]
    ppermute x1, starting transfers between devices: 3.44 us -> 4.43 us  [body(): theirs = lax.ppermute(mine, 'gy', swap)]
  transfers between devices with their start and end apart: 2 -> 6, of which waited for: 2 -> 5; matrix products, arithmetic and copies ran while one was open for 0% -> 0% of each run, Pallas kernels for 0% -> 0%
where the time goes in v4:
time: 49.7 us; the launch traced here: 49.6 us
  starting transfers between devices  16 us (32%)
  blocking collectives  14.1 us (28%)
  Pallas kernels  12.6 us (25%)
  waiting for transfers between devices  5.61 us (11%)
  between operations  1.33 us (3%)
    all_to_all x1, blocking collectives, body(): lax.all_to_all(call(pair_kernel, (ny // 2, *piece), mine, theirs), 'gy',...  14.1 us
    pallas_call x1, Pallas kernels, final_call(): pl.pallas_call(functools.partial(final_kernel, axis=axis), out_shape=(f32...  8.21 us
    ppermute x1, starting transfers between devices, body(): theirs = lax.ppermute(mine, 'gx', [(n, n ^ nx // 2) for n in range(nx)])  4.65 us
    ppermute x1, starting transfers between devices, body(): theirs = lax.ppermute(mine, 'gy', swap)  4.43 us
    pallas_call x1, Pallas kernels, gram_call(): pl.pallas_call(functools.partial(gram_kernel, axis=axis), out_shape=(f32(...  4.31 us
    ppermute x3, starting transfers between devices, body(): lax.ppermute(mine, 'gx', [(n, n ^ d) for n in range(nx)])  3.55 us
    ppermute x1, starting transfers between devices, body(): theirs = lax.ppermute(theirs, 'gy', swap)  3.33 us
    ppermute x3, waiting for transfers between devices, body(): lax.ppermute(mine, 'gx', [(n, n ^ d) for n in range(nx)])  2.59 us
  transfers between devices with their start and end apart: 6, of which 5 were waited for; matrix products, arithmetic and copies ran while one was open for 0% of the time, Pallas kernels for 0%

profile of v4, /device:TPU:1, one launch (start us, length us, event | category | flops | bytes accessed | tf_op | source)
XLA Modules:
  0.0 49.6 jit_solution(11204895383385778824)
XLA Ops:
  0.6 0.0 copy-start
  0.6 0.0 copy-start.1
  0.6 0.0 copy-start.2
  0.7 4.3 %shard_map.59 = (f32[40,128]{1,0:T(8,128)S(1)}, f32[40,128]{1,0:T(8,128)S(1)}) custom-call(bf16[128,128,128]{2,1,0:T(8,128)(2,1)} %data_ref.3), custom_call_target="tpu_custom_call" | custom-call | tf_op jit(solution)/shard_map/pallas_call | solution.py:214
  5.0 3.3 %collective-permute-start = (f32[40,128]{1,0:T(8,128)S(1)}, f32[40,128]{1,0:T(8,128)S(1)}, u32[]{:S(2)}, u32[]{:S(2)}) collective-permute-start(f32[40,128]{1,0:T(8,128)S(1)} %get-tuple-element.7), channel_id=1, source_target_pairs={{0,1},{1,0},{2,3},{3,2},{4,5},{5,4},{6,7},{7,6},{8,9},{9,8},{10,11... | collective-permute-start | bytes 61448 | tf_op jit(solution)/shard_map/ppermute | solution.py:259
  8.3 0.8 %collective-permute-done.refs_1_ = f32[40,128]{1,0:T(8,128)S(1)} collective-permute-done((f32[40,128]{1,0:T(8,128)S(1)}, f32[40,128]{1,0:T(8,128)S(1)}, u32[]{:S(2)}, u32[]{:S(2)}) %collective-permute-start) | collective-permute-done | bytes 20512 | tf_op jit(solution)/shard_map/ppermute | solution.py:259
  9.2 2.6 %collective-permute-start.3 = (f32[40,128]{1,0:T(8,128)S(1)}, f32[40,128]{1,0:T(8,128)S(1)}, u32[]{:S(2)}, u32[]{:S(2)}) collective-permute-start(f32[40,128]{1,0:T(8,128)S(1)} %shard_map.60.refs_0_), channel_id=1, source_target_pairs={{0,96},{32,64},{64,32},{96,0},{128,224},{160,192},{192,160},{224,1... | collective-permute-start | bytes 61448 | tf_op jit(solution)/shard_map/ppermute | solution.py:262
  11.8 0.0 collective-permute-start.2
  11.8 0.9 %collective-permute-start.1 = (f32[40,128]{1,0:T(8,128)S(1)}, f32[40,128]{1,0:T(8,128)S(1)}, u32[]{:S(2)}, u32[]{:S(2)}) collective-permute-start(f32[40,128]{1,0:T(8,128)S(1)} %shard_map.60.refs_0_), channel_id=1, source_target_pairs={{0,32},{32,0},{64,96},{96,64},{128,160},{160,128},{192,224},{224,1... | collective-permute-start | bytes 61448 | tf_op jit(solution)/shard_map/ppermute | solution.py:262
  12.7 0.9 %collective-permute-done.3.refs_3_ = f32[40,128]{1,0:T(8,128)S(1)} collective-permute-done((f32[40,128]{1,0:T(8,128)S(1)}, f32[40,128]{1,0:T(8,128)S(1)}, u32[]{:S(2)}, u32[]{:S(2)}) %collective-permute-start.3) | collective-permute-done | bytes 20512 | tf_op jit(solution)/shard_map/ppermute | solution.py:262
  13.6 1.7 %collective-permute-done.2.refs_2_ = f32[40,128]{1,0:T(8,128)S(1)} collective-permute-done((f32[40,128]{1,0:T(8,128)S(1)}, f32[40,128]{1,0:T(8,128)S(1)}, u32[]{:S(2)}, u32[]{:S(2)}) %collective-permute-start.2) | collective-permute-done | bytes 20512 | tf_op jit(solution)/shard_map/ppermute | solution.py:262
  15.3 0.0 collective-permute-done.1.refs_1_
  15.3 4.7 %collective-permute-start.4 = (f32[40,128]{1,0:T(8,128)S(1)}, f32[40,128]{1,0:T(8,128)S(1)}, u32[]{:S(2)}, u32[]{:S(2)}) collective-permute-start(f32[40,128]{1,0:T(8,128)S(1)} %shard_map.61.mine_ref), channel_id=1, source_target_pairs={{0,128},{32,160},{64,192},{96,224},{128,0},{160,32},{192,64},{224,... | collective-permute-start | bytes 61448 | tf_op jit(solution)/shard_map/ppermute | solution.py:264
  20.0 2.0 %collective-permute-done.4.theirs_ref = f32[40,128]{1,0:T(8,128)S(1)} collective-permute-done((f32[40,128]{1,0:T(8,128)S(1)}, f32[40,128]{1,0:T(8,128)S(1)}, u32[]{:S(2)}, u32[]{:S(2)}) %collective-permute-start.4) | collective-permute-done | bytes 20512 | tf_op jit(solution)/shard_map/ppermute | solution.py:264
  22.0 14.1 %all_to_all.5.in_ref = f32[16,9,4,128]{3,2,1,0:T(4,128)S(1)} all-to-all(f32[16,9,4,128]{3,2,1,0:T(4,128)S(1)} %shard_map.62), channel_id=1, replica_groups={{0,2,4,6,8,10,12,14,16,18,20,22,24,26,28,30},{1,3,5,7,9,11,13,15,17,19,..., dimensions={0} | all-to-all | bytes 589824 | tf_op jit(solution)/shard_map/all_to_all | solution.py:265
  36.1 4.4 %collective-permute-start.5 = (f32[40,128]{1,0:T(8,128)S(1)}, f32[40,128]{1,0:T(8,128)S(1)}, u32[]{:S(2)}, u32[]{:S(2)}) collective-permute-start(f32[40,128]{1,0:T(8,128)S(1)} %shard_map.63.mine_ref), channel_id=1, source_target_pairs={{0,1},{1,0},{2,3},{3,2},{4,5},{5,4},{6,7},{7,6},{8,9},{9,8},{10,11... | collective-permute-start | bytes 61448 | tf_op jit(solution)/shard_map/ppermute | solution.py:269
  41.2 0.2 collective-permute-done.5.theirs_ref
  41.4 0.0 copy-done
  41.4 0.0 copy-done.1
  41.4 0.0 copy-done.2
  41.4 8.2 %shard_map.64 = (f32[32,128]{1,0:T(8,128)}, bf16[32,128,128]{2,1,0:T(8,128)(2,1)}) custom-call(s32[1]{0:T(128)S(6)} %copy.6.rank_ref, f32[40,128]{1,0:T(8,128)S(1)} %shard_map.63.mine_ref, f32[40,128]{1,0:T(8,128)S(1)} %collective-permute-done.5.theirs_ref, f32[1,128]{1,0:T(1,128)S(1)} %bitcast.4, f32[32,128]{1,0:T(8,128)S(1)} %bitcast.3, ...), custom_call_target="tpu_custom_call" | custom-call | tf_op jit(solution)/shard_map/pallas_call | solution.py:231
  (4 shorter events, 0.1 us)
Async XLA Ops:
  0.6 40.8 %copy-start = (bf16[128,128,128]{2,1,0:T(8,128)(2,1)S(1)}, bf16[128,128,128]{2,1,0:T(8,128)(2,1)}, u32[]{:S(2)}) copy-start(bf16[128,128,128]{2,1,0:T(8,128)(2,1)} %data_ref.3) | copy-start | bytes 12582916
  0.6 40.7 %copy-start.1 = (f32[128,32]{0,1:T(8,128)S(1)}, f32[128,32]{0,1:T(8,128)}, u32[]{:S(2)}) copy-start(f32[128,32]{0,1:T(8,128)} %param.6) | copy-start | bytes 49156
  0.6 40.7 %copy-start.2 = (f32[128]{0:T(128)S(1)}, f32[128]{0:T(128)}, u32[]{:S(2)}) copy-start(f32[128]{0:T(128)} %param.5) | copy-start | bytes 1540
  5.0 4.2 %collective-permute-start = (f32[40,128]{1,0:T(8,128)S(1)}, f32[40,128]{1,0:T(8,128)S(1)}, u32[]{:S(2)}, u32[]{:S(2)}) collective-permute-start(f32[40,128]{1,0:T(8,128)S(1)} %get-tuple-element.7), channel_id=1, source_target_pairs={{0,1},{1,0},{2,3},{3,2},{4,5},{5,4},{6,7},{7,6},{8,9},{9,8},{10,11... | collective-permute-start | bytes 61448 | tf_op jit(solution)/shard_map/ppermute | solution.py:259
  9.2 4.4 %collective-permute-start.3 = (f32[40,128]{1,0:T(8,128)S(1)}, f32[40,128]{1,0:T(8,128)S(1)}, u32[]{:S(2)}, u32[]{:S(2)}) collective-permute-start(f32[40,128]{1,0:T(8,128)S(1)} %shard_map.60.refs_0_), channel_id=1, source_target_pairs={{0,96},{32,64},{64,32},{96,0},{128,224},{160,192},{192,160},{224,1... | collective-permute-start | bytes 61448 | tf_op jit(solution)/shard_map/ppermute | solution.py:262
  11.8 3.5 %collective-permute-start.2 = (f32[40,128]{1,0:T(8,128)S(1)}, f32[40,128]{1,0:T(8,128)S(1)}, u32[]{:S(2)}, u32[]{:S(2)}) collective-permute-start(f32[40,128]{1,0:T(8,128)S(1)} %shard_map.60.refs_0_), channel_id=1, source_target_pairs={{0,64},{32,96},{64,0},{96,32},{128,192},{160,224},{192,128},{224,1... | collective-permute-start | bytes 61448 | tf_op jit(solution)/shard_map/ppermute | solution.py:262
  11.8 3.5 %collective-permute-start.1 = (f32[40,128]{1,0:T(8,128)S(1)}, f32[40,128]{1,0:T(8,128)S(1)}, u32[]{:S(2)}, u32[]{:S(2)}) collective-permute-start(f32[40,128]{1,0:T(8,128)S(1)} %shard_map.60.refs_0_), channel_id=1, source_target_pairs={{0,32},{32,0},{64,96},{96,64},{128,160},{160,128},{192,224},{224,1... | collective-permute-start | bytes 61448 | tf_op jit(solution)/shard_map/ppermute | solution.py:262
  15.3 6.6 %collective-permute-start.4 = (f32[40,128]{1,0:T(8,128)S(1)}, f32[40,128]{1,0:T(8,128)S(1)}, u32[]{:S(2)}, u32[]{:S(2)}) collective-permute-start(f32[40,128]{1,0:T(8,128)S(1)} %shard_map.61.mine_ref), channel_id=1, source_target_pairs={{0,128},{32,160},{64,192},{96,224},{128,0},{160,32},{192,64},{224,... | collective-permute-start | bytes 61448 | tf_op jit(solution)/shard_map/ppermute | solution.py:264
  36.1 5.3 %collective-permute-start.5 = (f32[40,128]{1,0:T(8,128)S(1)}, f32[40,128]{1,0:T(8,128)S(1)}, u32[]{:S(2)}, u32[]{:S(2)}) collective-permute-start(f32[40,128]{1,0:T(8,128)S(1)} %shard_map.63.mine_ref), channel_id=1, source_target_pairs={{0,1},{1,0},{2,3},{3,2},{4,5},{5,4},{6,7},{7,6},{8,9},{9,8},{10,11... | collective-permute-start | bytes 61448 | tf_op jit(solution)/shard_map/ppermute | solution.py:269
